TPU v7x, 256 devices: a whole 4x4x8 slice. The times are simulated.
256 devices in a mesh: scene: 64 (over z_hi, y, x, core), view: 4 (over z_lo).
Axes of the slice: x: 4, y: 4, z: 8 (z_hi: 2, z_lo: 4; z = z_hi * 4 + z_lo), core: 2. Of those that a mesh axis runs over, the one named last changes fastest.
Arguments:
- queries: bfloat16 [64, 4, 512, 1024], P('scene', 'view'), may hold values from -6 to 6
- keys: bfloat16 [64, 4, 512, 1024], P('scene', 'view'), may hold values from -6 to 6
- values: bfloat16 [64, 4, 512, 1024], P('scene', 'view'), may hold values from -6 to 6
- out_grad: bfloat16 [64, 4, 512, 2048], P('scene', 'view'), may hold values from -1.5 to 1.5
- w_out: bfloat16 [1024, 2048], replicated, may hold values from -0.1875 to 0.1875
- bucket_of: int32 [64, 4, 4], P('scene'), may hold values from 0 to 3, as said below
- pair_mask: int32 [64, 4, 4], P('scene'), may hold values from 0 to 1, as said below
Outputs:
- layer_out: bfloat16 [64, 4, 512, 2048], P('scene', 'view')
- grad_queries: bfloat16 [64, 4, 512, 1024], P('scene', 'view')
- grad_keys: bfloat16 [64, 4, 512, 1024], P('scene', 'view')
- grad_values: bfloat16 [64, 4, 512, 1024], P('scene', 'view')
- grad_w_out: bfloat16 [1024, 2048], replicated
Inputs may be any that keep to these rules, and one draw needn't show every extreme that they name: `bucket_of`: each view's 4 blocks lie in 4 different buckets; in every scene one bucket holds a block of every view. pair_mask[s, a, a] = 1 for every view a.
All inputs are finite; a program needn't handle non-finite values.
Results may differ from a plain program's by a relative error of at most 0.008.
Values may be sent and summed in bfloat16 or wider, within the bound.
A program may use at most 128 MiB of HBM per device.

v0:
```python
import math
import jax
import jax.numpy as jnp
from jax import lax
from jax.sharding import PartitionSpec as P

HDIM = 128
BLK = 128
NEG_FILL = -1e30


def head_pass(inputs, allowed, inv_root):
    queries_h, keys_h, values_h, grads_h = inputs
    scores = (
        jnp.einsum("sid,sjd->sij", queries_h, keys_h, preferred_element_type=jnp.float32) * inv_root
    )
    scores = jnp.where(allowed, scores, NEG_FILL)
    peak = jnp.max(scores, axis=-1, keepdims=True)
    exponent = jnp.exp(scores - peak)
    weights = exponent / jnp.sum(exponent, axis=-1, keepdims=True)
    weights_b = weights.astype(jnp.bfloat16)
    attended = jnp.einsum(
        "sij,sjd->sid", weights_b, values_h, preferred_element_type=jnp.float32
    ).astype(jnp.bfloat16)
    grad_weights = jnp.einsum("sid,sjd->sij", grads_h, values_h, preferred_element_type=jnp.float32)
    row_dot = jnp.sum(weights * grad_weights, axis=-1, keepdims=True)
    grad_scores = (weights * (grad_weights - row_dot) * inv_root).astype(jnp.bfloat16)
    grad_query = jnp.einsum(
        "sij,sjd->sid", grad_scores, keys_h, preferred_element_type=jnp.float32
    ).astype(jnp.bfloat16)
    grad_key = jnp.einsum(
        "sij,sid->sjd", grad_scores, queries_h, preferred_element_type=jnp.float32
    ).astype(jnp.bfloat16)
    grad_value = jnp.einsum(
        "sij,sid->sjd", weights_b, grads_h, preferred_element_type=jnp.float32
    ).astype(jnp.bfloat16)
    return (attended, grad_query, grad_key, grad_value)


def body(queries, keys, values, out_grad, w_out, bucket_of, pair_mask):
    view_count = lax.axis_size("view")
    owner_id = lax.axis_index("view")
    scenes_here = queries.shape[0]
    tokens = queries.shape[2]
    width = queries.shape[3]
    heads = width // HDIM
    block_count = tokens // BLK
    rows_all = view_count * BLK
    dest_ids = jnp.arange(view_count, dtype=jnp.int32)
    my_buckets = lax.dynamic_index_in_dim(bucket_of, owner_id, 1, keepdims=False)
    selector = (my_buckets[:, None, :] == dest_ids[None, :, None]).astype(jnp.bfloat16)

    def pack(tensor):
        blocks = tensor.reshape(scenes_here, block_count, BLK, tensor.shape[-1])
        return jnp.einsum(
            "sdb,sbrf->sdrf", selector, blocks, preferred_element_type=jnp.float32
        ).astype(jnp.bfloat16)

    def unpack(tensor):
        blocks = jnp.einsum(
            "sdb,sdrf->sbrf", selector, tensor, preferred_element_type=jnp.float32
        ).astype(jnp.bfloat16)
        return blocks.reshape(scenes_here, 1, tokens, tensor.shape[-1])

    grad_attn = jnp.einsum(
        "svtd,fd->svtf", out_grad, w_out, preferred_element_type=jnp.float32
    ).astype(jnp.bfloat16)
    got_query, got_key, got_value, got_grad = (
        lax.all_to_all(pack(queries), "view", split_axis=1, concat_axis=1, tiled=True),
        lax.all_to_all(pack(keys), "view", split_axis=1, concat_axis=1, tiled=True),
        lax.all_to_all(pack(values), "view", split_axis=1, concat_axis=1, tiled=True),
        lax.all_to_all(pack(grad_attn), "view", split_axis=1, concat_axis=1, tiled=True),
    )
    live_src = jnp.any(bucket_of == owner_id, axis=2)
    allowed_blocks = (pair_mask > 0) & live_src[:, None, :]
    allowed = jnp.repeat(jnp.repeat(allowed_blocks, BLK, axis=1), BLK, axis=2)
    inv_root = 1.0 / math.sqrt(HDIM)

    def split_heads(tensor):
        return tensor.reshape(scenes_here, rows_all, heads, HDIM).transpose(2, 0, 1, 3)

    def join_heads(tensor):
        return tensor.transpose(1, 2, 0, 3).reshape(scenes_here, view_count, BLK, width)

    results = lax.map(
        lambda inputs: head_pass(inputs, allowed, inv_root),
        (
            split_heads(got_query),
            split_heads(got_key),
            split_heads(got_value),
            split_heads(got_grad),
        ),
    )
    back_attended, back_query, back_key, back_value = (
        lax.all_to_all(join_heads(results[0]), "view", split_axis=1, concat_axis=1, tiled=True),
        lax.all_to_all(join_heads(results[1]), "view", split_axis=1, concat_axis=1, tiled=True),
        lax.all_to_all(join_heads(results[2]), "view", split_axis=1, concat_axis=1, tiled=True),
        lax.all_to_all(join_heads(results[3]), "view", split_axis=1, concat_axis=1, tiled=True),
    )
    attended = unpack(back_attended)
    grad_queries = unpack(back_query)
    grad_keys = unpack(back_key)
    grad_values = unpack(back_value)
    layer_out = jnp.einsum(
        "svtf,fd->svtd", attended, w_out, preferred_element_type=jnp.float32
    ).astype(jnp.bfloat16)
    partial_grad = jnp.einsum(
        "svtf,svtd->fd", attended, out_grad, preferred_element_type=jnp.float32
    )
    grad_w_out = lax.psum(partial_grad, ("scene", "view")).astype(jnp.bfloat16)
    return (layer_out, grad_queries, grad_keys, grad_values, grad_w_out)


def solution(mesh):
    placed = (
        P("scene", "view", None, None),
        P("scene", "view", None, None),
        P("scene", "view", None, None),
        P("scene", "view", None, None),
        P(),
        P("scene", None, None),
        P("scene", None, None),
    )
    return jax.shard_map(
        body,
        mesh=mesh,
        in_specs=placed,
        out_specs=(
            P("scene", "view", None, None),
            P("scene", "view", None, None),
            P("scene", "view", None, None),
            P("scene", "view", None, None),
            P(),
        ),
        check_vma=False,
    )
```

profile of v0, /device:TPU:1, one launch (start us, length us, event | category | flops | bytes accessed | tf_op | source)
XLA Modules:
  0.0 468.7 jit_solution(9484183739912808766)
XLA Ops:
  2.2 4.5 fusion.45
  9.4 6.4 %all-to-all-start.3 = ((bf16[1,4,128,1024]{3,2,0,1:T(8,128)(2,1)}), bf16[1,4,128,1024]{3,2,0,1:T(8,128)(2,1)S(1)}, u32[]{:S(2)}, u32[]{:S(2)}) async-start(bf16[1,4,128,1024]{3,2,0,1:T(8,128)(2,1)} %copy.61), calls=%async_computation.3 | async-start | bytes 2097152 | tf_op jit(solution)/shard_map/all_to_all | solution.py:72
  15.9 2.4 fusion.48
  19.5 21.6 %all-to-all-done.3 = bf16[1,4,128,1024]{3,2,0,1:T(8,128)(2,1)S(1)} async-done(((bf16[1,4,128,1024]{3,2,0,1:T(8,128)(2,1)}), bf16[1,4,128,1024]{3,2,0,1:T(8,128)(2,1)S(1)}, u32[]{:S(2)}, u32[]{:S(2)}) %all-to-all-start.3) | async-done | bytes 1048608 | tf_op jit(solution)/shard_map/all_to_all | solution.py:72
  41.1 4.3 all-to-all-start
  45.4 2.4 fusion.49
  49.0 21.6 %all-to-all-done = bf16[1,4,128,1024]{3,2,0,1:T(8,128)(2,1)} async-done(((bf16[1,4,128,1024]{3,2,0,1:T(8,128)(2,1)}), bf16[1,4,128,1024]{3,2,0,1:T(8,128)(2,1)}, u32[]{:S(2)}, u32[]{:S(2)}) %all-to-all-start) | async-done | bytes 1048608 | tf_op jit(solution)/shard_map/all_to_all | solution.py:69
  70.6 4.2 all-to-all-start.1
  74.9 2.4 fusion.50
  78.6 21.6 %all-to-all-done.1 = bf16[1,4,128,1024]{3,2,0,1:T(8,128)(2,1)} async-done(((bf16[1,4,128,1024]{3,2,0,1:T(8,128)(2,1)}), bf16[1,4,128,1024]{3,2,0,1:T(8,128)(2,1)}, u32[]{:S(2)}, u32[]{:S(2)}) %all-to-all-start.1) | async-done | bytes 1048608 | tf_op jit(solution)/shard_map/all_to_all | solution.py:70
  100.2 4.4 all-to-all-start.2
  110.9 18.8 %all-to-all-done.2 = bf16[1,4,128,1024]{3,2,0,1:T(8,128)(2,1)} async-done(((bf16[1,4,128,1024]{3,2,0,1:T(8,128)(2,1)}), bf16[1,4,128,1024]{3,2,0,1:T(8,128)(2,1)}, u32[]{:S(2)}, u32[]{:S(2)}) %all-to-all-start.2) | async-done | bytes 1048608 | tf_op jit(solution)/shard_map/all_to_all | solution.py:71
  132.5 78.6 %while.17 = (s32[]{:T(128)}, bf16[8,1,512,128]{3,2,1,0:T(8,128)(2,1)}, bf16[8,1,512,128]{3,2,1,0:T(8,128)(2,1)}, bf16[8,1,512,128]{3,2,1,0:T(8,128)(2,1)}, bf16[...) while((s32[]{:T(128)}, ...), condition=%wide.region_5.6_spmd.clone, body=%wide.region_1.5_spmd.clone.sunk | while | flops 408418816 | bytes 12093549 | solution.py:85
  140.3 1.9 fusion.104
  150.2 1.9 fusion.104
  160.0 1.9 fusion.104
  189.5 1.9 fusion.104
  209.1 1.9 fusion.104
  214.3 4.2 all-to-all-start.4
  221.7 22.1 %all-to-all-done.4 = bf16[1,4,128,1024]{3,2,0,1:T(8,128)(2,1)} async-done(((bf16[1,4,128,1024]{3,2,0,1:T(8,128)(2,1)}), bf16[1,4,128,1024]{3,2,0,1:T(8,128)(2,1)}, u32[]{:S(2)}, u32[]{:S(2)}) %all-to-all-start.4) | async-done | bytes 1048608 | tf_op jit(solution)/shard_map/all_to_all | solution.py:95
  243.8 4.3 all-to-all-start.5
  251.2 22.1 %all-to-all-done.5 = bf16[1,4,128,1024]{3,2,0,1:T(8,128)(2,1)} async-done(((bf16[1,4,128,1024]{3,2,0,1:T(8,128)(2,1)}), bf16[1,4,128,1024]{3,2,0,1:T(8,128)(2,1)}, u32[]{:S(2)}, u32[]{:S(2)}) %all-to-all-start.5) | async-done | bytes 1048608 | tf_op jit(solution)/shard_map/all_to_all | solution.py:96
  273.3 4.2 all-to-all-start.6
  280.8 2.2 convolution_convert_fusion.8
  283.3 5.6 %fusion.41 = f32[1024,2048]{1,0:T(8,128)} fusion(bf16[512,1024]{1,0:T(8,128)(2,1)S(1)} %bitcast.215, bf16[1,1,512,2048]{3,2,1,0:T(8,128)(2,1)S(1)} %copy-done), kind=kOutput, calls=%fused_computation.47 | convolution fusion | flops 2147483648 | bytes 11534336 | tf_op jit(solution)/shard_map/svtf,svtd->fd/dot_general | solution.py:107
  288.9 14.0 %all-to-all-done.6 = bf16[1,4,128,1024]{3,2,0,1:T(8,128)(2,1)} async-done(((bf16[1,4,128,1024]{3,2,0,1:T(8,128)(2,1)}), bf16[1,4,128,1024]{3,2,0,1:T(8,128)(2,1)}, u32[]{:S(2)}, u32[]{:S(2)}) %all-to-all-start.6) | async-done | bytes 1048608 | tf_op jit(solution)/shard_map/all_to_all | solution.py:97
  302.9 4.2 all-to-all-start.7
  307.1 147.3 %all-reduce.1 = bf16[1024,2048]{1,0:T(8,128)(2,1)} all-reduce(f32[1024,2048]{1,0:T(8,128)} %fusion.41), channel_id=1, replica_groups=mesh['scene'=64,'view'=4] {'scene','view'}, use_global_device_ids=true, to_apply=%region_6.7 | all-reduce | flops 2097152 | bytes 12582912 | tf_op jit(solution)/shard_map/psum | solution.py:110
  454.4 2.2 convolution_convert_fusion.7
  457.9 2.3 convolution_convert_fusion.6
  461.5 3.7 fusion.40
  465.2 2.2 convolution_convert_fusion.5
  (115 shorter events, 102.7 us)
Async XLA Ops:
  0.6 1.6 copy-start
  9.4 31.7 %all-to-all-start.3 = ((bf16[1,4,128,1024]{3,2,0,1:T(8,128)(2,1)}), bf16[1,4,128,1024]{3,2,0,1:T(8,128)(2,1)S(1)}, u32[]{:S(2)}, u32[]{:S(2)}) async-start(bf16[1,4,128,1024]{3,2,0,1:T(8,128)(2,1)} %copy.61), calls=%async_computation.3 | async-start | bytes 2097152 | tf_op jit(solution)/shard_map/all_to_all | solution.py:72
  41.1 29.5 %all-to-all-start = ((bf16[1,4,128,1024]{3,2,0,1:T(8,128)(2,1)}), bf16[1,4,128,1024]{3,2,0,1:T(8,128)(2,1)}, u32[]{:S(2)}, u32[]{:S(2)}) async-start(bf16[1,4,128,1024]{3,2,0,1:T(8,128)(2,1)} %copy.52), calls=%async_computation | async-start | bytes 2097152 | tf_op jit(solution)/shard_map/all_to_all | solution.py:69
  70.6 29.5 %all-to-all-start.1 = ((bf16[1,4,128,1024]{3,2,0,1:T(8,128)(2,1)}), bf16[1,4,128,1024]{3,2,0,1:T(8,128)(2,1)}, u32[]{:S(2)}, u32[]{:S(2)}) async-start(bf16[1,4,128,1024]{3,2,0,1:T(8,128)(2,1)} %copy.55), calls=%async_computation.1 | async-start | bytes 2097152 | tf_op jit(solution)/shard_map/all_to_all | solution.py:70
  77.3 27.4 %copy-start.1 = (s32[1,4,4]{2,1,0:T(4,128)S(1)}, s32[1,4,4]{2,1,0:T(4,128)}, u32[]{:S(2)}) copy-start(s32[1,4,4]{2,1,0:T(4,128)} %param.14) | copy-start | bytes 196
  77.3 27.5 %copy-start.2 = (s32[1,4,4]{2,1,0:T(4,128)S(1)}, s32[1,4,4]{2,1,0:T(4,128)}, u32[]{:S(2)}) copy-start(s32[1,4,4]{2,1,0:T(4,128)} %param.15) | copy-start | bytes 196
  100.2 29.5 %all-to-all-start.2 = ((bf16[1,4,128,1024]{3,2,0,1:T(8,128)(2,1)}), bf16[1,4,128,1024]{3,2,0,1:T(8,128)(2,1)}, u32[]{:S(2)}, u32[]{:S(2)}) async-start(bf16[1,4,128,1024]{3,2,0,1:T(8,128)(2,1)} %copy.58), calls=%async_computation.2 | async-start | bytes 2097152 | tf_op jit(solution)/shard_map/all_to_all | solution.py:71
  214.3 29.5 %all-to-all-start.4 = ((bf16[1,4,128,1024]{3,2,0,1:T(8,128)(2,1)}), bf16[1,4,128,1024]{3,2,0,1:T(8,128)(2,1)}, u32[]{:S(2)}, u32[]{:S(2)}) async-start(bf16[1,4,128,1024]{3,2,0,1:T(8,128)(2,1)} %bitcast.21), calls=%async_computation.4 | async-start | bytes 2097152 | tf_op jit(solution)/shard_map/all_to_all | solution.py:95
  243.8 29.5 %all-to-all-start.5 = ((bf16[1,4,128,1024]{3,2,0,1:T(8,128)(2,1)}), bf16[1,4,128,1024]{3,2,0,1:T(8,128)(2,1)}, u32[]{:S(2)}, u32[]{:S(2)}) async-start(bf16[1,4,128,1024]{3,2,0,1:T(8,128)(2,1)} %bitcast.26), calls=%async_computation.5 | async-start | bytes 2097152 | tf_op jit(solution)/shard_map/all_to_all | solution.py:96
  273.3 29.5 %all-to-all-start.6 = ((bf16[1,4,128,1024]{3,2,0,1:T(8,128)(2,1)}), bf16[1,4,128,1024]{3,2,0,1:T(8,128)(2,1)}, u32[]{:S(2)}, u32[]{:S(2)}) async-start(bf16[1,4,128,1024]{3,2,0,1:T(8,128)(2,1)} %bitcast.30), calls=%async_computation.6 | async-start | bytes 2097152 | tf_op jit(solution)/shard_map/all_to_all | solution.py:97
  302.9 162.4 %all-to-all-start.7 = ((bf16[1,4,128,1024]{3,2,0,1:T(8,128)(2,1)}), bf16[1,4,128,1024]{3,2,0,1:T(8,128)(2,1)}, u32[]{:S(2)}, u32[]{:S(2)}) async-start(bf16[1,4,128,1024]{3,2,0,1:T(8,128)(2,1)} %bitcast.34), calls=%async_computation.7 | async-start | bytes 2097152 | tf_op jit(solution)/shard_map/all_to_all | solution.py:98
  457.9 3.6 copy-start.3
where the time goes:
time: 471 us; the launch traced here: 469 us
  blocking collectives  147 us (31%)
  waiting for transfers between devices  142 us (30%)
  matrix products  105 us (22%)
  starting transfers between devices  36.4 us (8%)
  local copies, waits for them, and re-layouts  33 us (7%)
    psum x1, blocking collectives, body(): grad_w_out = lax.psum(partial_grad, ('scene', 'view')).astype(jnp.bfloat16)  147 us
    all_to_all x1, waiting for transfers between devices, body(): lax.all_to_all(join_heads(results[0]), 'view', split_axis=1, concat_axis=...  22.1 us
    all_to_all x1, waiting for transfers between devices, body(): lax.all_to_all(join_heads(results[1]), 'view', split_axis=1, concat_axis=...  22.1 us
    all_to_all x1, waiting for transfers between devices, body(): lax.all_to_all(pack(queries), 'view', split_axis=1, concat_axis=1, tiled=...  21.6 us
    all_to_all x1, waiting for transfers between devices, body(): lax.all_to_all(pack(keys), 'view', split_axis=1, concat_axis=1, tiled=True)  21.6 us
    all_to_all x1, waiting for transfers between devices, body(): lax.all_to_all(pack(grad_attn), 'view', split_axis=1, concat_axis=1, tile...  21.6 us
    all_to_all x1, waiting for transfers between devices, body(): lax.all_to_all(pack(values), 'view', split_axis=1, concat_axis=1, tiled=T...  18.8 us
    dot_general x8, matrix products, head_pass(): jnp.einsum('sij,sjd->sid', weights_b, values_h, preferred_element_type=jn...  15.5 us
  transfers between devices with their start and end apart: 8, of which 7 were waited for; matrix products, arithmetic and copies ran while one was open for 10% of the time, Pallas kernels for 0%

commit v1 on v0

--- a/solution.py
+++ b/solution.py
@@ -107,7 +107,7 @@
     partial_grad = jnp.einsum(
         "svtf,svtd->fd", attended, out_grad, preferred_element_type=jnp.float32
     )
-    grad_w_out = lax.psum(partial_grad, ("scene", "view")).astype(jnp.bfloat16)
+    grad_w_out = lax.psum(lax.psum(partial_grad, "scene"), "view").astype(jnp.bfloat16)
     return (layer_out, grad_queries, grad_keys, grad_values, grad_w_out)
 
 

time: 471 us -> 1380 us (2.93)
  waiting for transfers between devices: 142 us -> 879 us
  blocking collectives: 147 us -> 307 us
    psum x0 -> x1, waiting for transfers between devices: none -> 718 us  [body(): lax.psum(partial_grad, 'scene')]
    psum x1, blocking collectives: 147 us -> 278 us  [body(): lax.psum(lax.psum(partial_grad, 'scene'), 'view').astype(jnp.bfloat16)]
    all_to_all x0 -> x1, blocking collectives: none -> 28.3 us  [body(): lax.all_to_all(join_heads(results[0]), 'view', split_axis=1, concat_axis=...]
    all_to_all x1, waiting for transfers between devices: 0.01 us -> 23.4 us  [body(): lax.all_to_all(join_heads(results[3]), 'view', split_axis=1, concat_axis=...]
    all_to_all x1 -> x0, waiting for transfers between devices: 22.1 us -> none  [body(): lax.all_to_all(join_heads(results[0]), 'view', split_axis=1, concat_axis=...]
  transfers between devices with their start and end apart: 8 -> 8, of which waited for: 7 -> 8; matrix products, arithmetic and copies ran while one was open for 10% -> 3% of each run, Pallas kernels for 0% -> 0%
where the time goes in v1:
time: 1380 us
  waiting for transfers between devices  879 us (64%)
  blocking collectives  307 us (22%)
  matrix products  106 us (8%)
  local copies, waits for them, and re-layouts  34 us (2%)
  starting transfers between devices  32.3 us (2%)
  between operations  14.3 us (1%)
    psum x1, waiting for transfers between devices, body(): lax.psum(partial_grad, 'scene')  718 us
    psum x1, blocking collectives, body(): lax.psum(lax.psum(partial_grad, 'scene'), 'view').astype(jnp.bfloat16)  278 us
    all_to_all x1, blocking collectives, body(): lax.all_to_all(join_heads(results[0]), 'view', split_axis=1, concat_axis=...  28.3 us
    all_to_all x1, waiting for transfers between devices, body(): lax.all_to_all(join_heads(results[2]), 'view', split_axis=1, concat_axis=...  27.7 us
  transfers between devices with their start and end apart: 8, of which 8 were waited for; matrix products, arithmetic and copies ran while one was open for 3% of the time, Pallas kernels for 0%

profile of v1, /device:TPU:1, one launch (start us, length us, event | category | flops | bytes accessed | tf_op | source)
XLA Modules:
  0.0 1375.9 jit_solution(3952468451164872313)
XLA Ops:
  8.8 4.5 fusion.45
  15.9 6.4 all-to-all-start.3
  22.4 2.4 fusion.48
  26.0 21.6 %all-to-all-done.3 = bf16[1,4,128,1024]{3,2,0,1:T(8,128)(2,1)S(1)} async-done(((bf16[1,4,128,1024]{3,2,0,1:T(8,128)(2,1)}), bf16[1,4,128,1024]{3,2,0,1:T(8,128)(2,1)S(1)}, u32[]{:S(2)}, u32[]{:S(2)}) %all-to-all-start.3) | async-done | bytes 1048608 | tf_op jit(solution)/shard_map/all_to_all | solution.py:72
  47.6 4.2 all-to-all-start
  51.9 2.4 fusion.49
  55.5 21.6 %all-to-all-done = bf16[1,4,128,1024]{3,2,0,1:T(8,128)(2,1)} async-done(((bf16[1,4,128,1024]{3,2,0,1:T(8,128)(2,1)}), bf16[1,4,128,1024]{3,2,0,1:T(8,128)(2,1)}, u32[]{:S(2)}, u32[]{:S(2)}) %all-to-all-start) | async-done | bytes 1048608 | tf_op jit(solution)/shard_map/all_to_all | solution.py:69
  77.1 4.2 all-to-all-start.1
  81.4 2.4 fusion.50
  85.1 21.6 %all-to-all-done.1 = bf16[1,4,128,1024]{3,2,0,1:T(8,128)(2,1)} async-done(((bf16[1,4,128,1024]{3,2,0,1:T(8,128)(2,1)}), bf16[1,4,128,1024]{3,2,0,1:T(8,128)(2,1)}, u32[]{:S(2)}, u32[]{:S(2)}) %all-to-all-start.1) | async-done | bytes 1048608 | tf_op jit(solution)/shard_map/all_to_all | solution.py:70
  106.7 4.2 all-to-all-start.2
  117.5 18.7 %all-to-all-done.2 = bf16[1,4,128,1024]{3,2,0,1:T(8,128)(2,1)} async-done(((bf16[1,4,128,1024]{3,2,0,1:T(8,128)(2,1)}), bf16[1,4,128,1024]{3,2,0,1:T(8,128)(2,1)}, u32[]{:S(2)}, u32[]{:S(2)}) %all-to-all-start.2) | async-done | bytes 1048608 | tf_op jit(solution)/shard_map/all_to_all | solution.py:71
  139.0 78.6 %while.17 = (s32[]{:T(128)}, bf16[8,1,512,128]{3,2,1,0:T(8,128)(2,1)}, bf16[8,1,512,128]{3,2,1,0:T(8,128)(2,1)}, bf16[8,1,512,128]{3,2,1,0:T(8,128)(2,1)}, bf16[...) while((s32[]{:T(128)}, ...), condition=%wide.region_5.6_spmd.clone, body=%wide.region_1.5_spmd.clone.sunk | while | flops 408418816 | bytes 12093549 | solution.py:85
  146.9 1.9 fusion.104
  156.7 1.9 fusion.104
  176.3 1.9 fusion.104
  196.0 1.9 fusion.104
  205.8 1.9 fusion.104
  220.8 28.3 %all_to_all.40 = bf16[1,4,128,1024]{3,2,0,1:T(8,128)(2,1)S(1)} all-to-all(bf16[1,4,128,1024]{3,2,0,1:T(8,128)(2,1)} %bitcast.207), channel_id=1, replica_groups=mesh['scene'=64,'view'=4] {'view'}, dimensions={1} | all-to-all | bytes 2097152 | tf_op jit(solution)/shard_map/all_to_all | solution.py:95
  251.3 5.6 fusion.41
  260.1 4.2 all-to-all-start.5
  267.6 26.0 %all-to-all-done.5 = bf16[1,4,128,1024]{3,2,0,1:T(8,128)(2,1)} async-done(((bf16[1,4,128,1024]{3,2,0,1:T(8,128)(2,1)}), bf16[1,4,128,1024]{3,2,0,1:T(8,128)(2,1)}, u32[]{:S(2)}, u32[]{:S(2)}) %all-to-all-start.5) | async-done | bytes 1048608 | tf_op jit(solution)/shard_map/all_to_all | solution.py:96
  293.6 4.2 all-to-all-start.6
  301.0 27.7 %all-to-all-done.6 = bf16[1,4,128,1024]{3,2,0,1:T(8,128)(2,1)} async-done(((bf16[1,4,128,1024]{3,2,0,1:T(8,128)(2,1)}), bf16[1,4,128,1024]{3,2,0,1:T(8,128)(2,1)}, u32[]{:S(2)}, u32[]{:S(2)}) %all-to-all-start.6) | async-done | bytes 1048608 | tf_op jit(solution)/shard_map/all_to_all | solution.py:97
  328.7 4.5 all-to-all-start.7
  333.2 2.2 convolution_convert_fusion.7
  336.7 2.2 convolution_convert_fusion.6
  340.1 23.4 %all-to-all-done.7 = bf16[1,4,128,1024]{3,2,0,1:T(8,128)(2,1)} async-done(((bf16[1,4,128,1024]{3,2,0,1:T(8,128)(2,1)}), bf16[1,4,128,1024]{3,2,0,1:T(8,128)(2,1)}, u32[]{:S(2)}, u32[]{:S(2)}) %all-to-all-start.7) | async-done | bytes 1048608 | tf_op jit(solution)/shard_map/all_to_all | solution.py:98
  363.6 2.2 convolution_convert_fusion.5
  367.0 5.9 fusion.40
  372.9 717.8 %all-reduce.3.cloned.1.call-done = f32[1024,2048]{1,0:T(8,128)} async-done(((f32[1024,2048]{1,0:T(8,128)}), f32[1024,2048]{1,0:T(8,128)}) %all-reduce.3.cloned.1.call-update) | async-done | bytes 8388624 | tf_op jit(solution)/shard_map/psum | solution.py:110
  1090.7 278.3 %all-reduce.4 = bf16[1024,2048]{1,0:T(8,128)(2,1)} all-reduce(f32[1024,2048]{1,0:T(8,128)} %all-reduce.3.cloned.1.call-done), channel_id=1, replica_groups=mesh['scene'=64,'view'=4] {'view'}, use_global_device_ids=true, to_apply=%region_7.8 | all-reduce | flops 2097152 | bytes 12582912 | tf_op jit(solution)/shard_map/psum | solution.py:110
  (119 shorter events, 104.9 us)
Async XLA Ops:
  7.2 1.6 copy-start
  15.9 31.7 %all-to-all-start.3 = ((bf16[1,4,128,1024]{3,2,0,1:T(8,128)(2,1)}), bf16[1,4,128,1024]{3,2,0,1:T(8,128)(2,1)S(1)}, u32[]{:S(2)}, u32[]{:S(2)}) async-start(bf16[1,4,128,1024]{3,2,0,1:T(8,128)(2,1)} %copy.61), calls=%async_computation.3 | async-start | bytes 2097152 | tf_op jit(solution)/shard_map/all_to_all | solution.py:72
  47.6 29.5 %all-to-all-start = ((bf16[1,4,128,1024]{3,2,0,1:T(8,128)(2,1)}), bf16[1,4,128,1024]{3,2,0,1:T(8,128)(2,1)}, u32[]{:S(2)}, u32[]{:S(2)}) async-start(bf16[1,4,128,1024]{3,2,0,1:T(8,128)(2,1)} %copy.52), calls=%async_computation | async-start | bytes 2097152 | tf_op jit(solution)/shard_map/all_to_all | solution.py:69
  77.1 29.5 %all-to-all-start.1 = ((bf16[1,4,128,1024]{3,2,0,1:T(8,128)(2,1)}), bf16[1,4,128,1024]{3,2,0,1:T(8,128)(2,1)}, u32[]{:S(2)}, u32[]{:S(2)}) async-start(bf16[1,4,128,1024]{3,2,0,1:T(8,128)(2,1)} %copy.55), calls=%async_computation.1 | async-start | bytes 2097152 | tf_op jit(solution)/shard_map/all_to_all | solution.py:70
  83.8 27.4 %copy-start.3 = (s32[1,4,4]{2,1,0:T(4,128)S(1)}, s32[1,4,4]{2,1,0:T(4,128)}, u32[]{:S(2)}) copy-start(s32[1,4,4]{2,1,0:T(4,128)} %param.14) | copy-start | bytes 196
  83.8 27.5 %copy-start.4 = (s32[1,4,4]{2,1,0:T(4,128)S(1)}, s32[1,4,4]{2,1,0:T(4,128)}, u32[]{:S(2)}) copy-start(s32[1,4,4]{2,1,0:T(4,128)} %param.15) | copy-start | bytes 196
  106.7 29.5 %all-to-all-start.2 = ((bf16[1,4,128,1024]{3,2,0,1:T(8,128)(2,1)}), bf16[1,4,128,1024]{3,2,0,1:T(8,128)(2,1)}, u32[]{:S(2)}, u32[]{:S(2)}) async-start(bf16[1,4,128,1024]{3,2,0,1:T(8,128)(2,1)} %copy.58), calls=%async_computation.2 | async-start | bytes 2097152 | tf_op jit(solution)/shard_map/all_to_all | solution.py:71
  110.9 979.8 %all-reduce.3.cloned.1.call-start = ((), (), s32[]{:S(2)}) async-start(), calls=%async_computation.8 | async-start | bytes 16777216 | tf_op jit(solution)/shard_map/psum | solution.py:110
  250.3 1.0 copy-start.1
  260.1 33.4 %all-to-all-start.5 = ((bf16[1,4,128,1024]{3,2,0,1:T(8,128)(2,1)}), bf16[1,4,128,1024]{3,2,0,1:T(8,128)(2,1)}, u32[]{:S(2)}, u32[]{:S(2)}) async-start(bf16[1,4,128,1024]{3,2,0,1:T(8,128)(2,1)} %bitcast.26), calls=%async_computation.5 | async-start | bytes 2097152 | tf_op jit(solution)/shard_map/all_to_all | solution.py:96
  293.6 35.2 %all-to-all-start.6 = ((bf16[1,4,128,1024]{3,2,0,1:T(8,128)(2,1)}), bf16[1,4,128,1024]{3,2,0,1:T(8,128)(2,1)}, u32[]{:S(2)}, u32[]{:S(2)}) async-start(bf16[1,4,128,1024]{3,2,0,1:T(8,128)(2,1)} %bitcast.30), calls=%async_computation.6 | async-start | bytes 2097152 | tf_op jit(solution)/shard_map/all_to_all | solution.py:97
  328.7 34.8 %all-to-all-start.7 = ((bf16[1,4,128,1024]{3,2,0,1:T(8,128)(2,1)}), bf16[1,4,128,1024]{3,2,0,1:T(8,128)(2,1)}, u32[]{:S(2)}, u32[]{:S(2)}) async-start(bf16[1,4,128,1024]{3,2,0,1:T(8,128)(2,1)} %bitcast.34), calls=%async_computation.7 | async-start | bytes 2097152 | tf_op jit(solution)/shard_map/all_to_all | solution.py:98
  340.1 26.9 %copy-start.2 = (bf16[4,128,1024]{2,1,0:T(8,128)(2,1)S(1)}, bf16[4,128,1024]{2,1,0:T(8,128)(2,1)}, u32[]{:S(2)}) copy-start(bf16[4,128,1024]{2,1,0:T(8,128)(2,1)} %copy-done.1) | copy-start | bytes 3145732
Sparse Core Ops, SparseCore 0:
  257.1 833.6 all-reduce.2
